TPU v7x, 256 devices: a whole 4x4x8 slice. The times are simulated.
256 devices in a mesh: tm: 4 (over x_hi, core), rows: 32 (over z, y), clip: 2 (over x_lo).
Axes of the slice: x: 4 (x_hi: 2, x_lo: 2; x = x_hi * 2 + x_lo), y: 4, z: 8, core: 2. Of those that a mesh axis runs over, the one named last changes fastest.
Arguments:
- video: bfloat16 [2, 16, 64, 128, 384], P('clip', 'tm', 'rows'), may hold values from -8 to 8
- leading_norm_gain: float32 [96], replicated, may hold values from 0.1 to 1.9
- conv_first: bfloat16 [3, 3, 3, 96, 96], replicated, may hold values from -0.125 to 0.125
- strided_down_kernel: bfloat16 [3, 3, 96, 96], replicated, may hold values from -0.21875 to 0.21875
- gain_second: float32 [96], replicated, may hold values from 0.1 to 1.9
- conv_second: bfloat16 [3, 3, 3, 96, 192], replicated, may hold values from -0.125 to 0.125
- shortcut: bfloat16 [96, 192], replicated, may hold values from -0.625 to 0.625
Outputs:
- latents: bfloat16 [2, 16, 32, 64, 768], P(None, 'tm', None, ('rows', 'clip'))
All inputs are finite; a program needn't handle non-finite values.
Results may differ from a plain program's by a relative error of at most 0.0058.
Values may be sent and summed in bfloat16 or wider, within the bound.
A program may use at most 128 MiB of HBM per device.

v0:
```python
import functools

import jax
import jax.numpy as jnp
from jax import lax
from jax.experimental import pallas as pl
from jax.experimental.pallas import tpu as pltpu
from jax.sharding import PartitionSpec as P

MESH = pl.DeviceIdType.MESH
F32 = jnp.float32
BF16 = jnp.bfloat16
VMEM_LIMIT = 56 * 1024 * 1024


def iota2(shape, dim):
    return lax.broadcasted_iota(jnp.int32, shape, dim)


def selector(rows, cols, offset):
    return jnp.where(iota2((rows, cols), 1) == iota2((rows, cols), 0) + offset, 1.0, 0.0).astype(BF16)


def dot(a, b):
    return jnp.dot(a, b, preferred_element_type=F32)


def place_exact(vector, chosen):
    wide = jnp.broadcast_to(vector, (8, vector.shape[1]))
    high = wide.astype(BF16)
    rest = wide - high.astype(F32)
    middle = rest.astype(BF16)
    low = (rest - middle.astype(F32)).astype(BF16)
    return (dot(high, chosen) + dot(middle, chosen) + dot(low, chosen))[0:1]


def squares_split(values):
    square = values * values
    high = square.astype(BF16)
    low = (square - high.astype(F32)).astype(BF16)
    return jnp.concatenate([high, low], 1)


def normsilu(values, meansq, half_gain):
    half = values * lax.rsqrt(meansq + 1e-6) * half_gain
    return half + half * jnp.tanh(half)


def shift_down(x):
    moved = pltpu.roll(x, 1, 0)
    return jnp.where(iota2(x.shape, 0) == 0, 0.0, moved)


def shift_up(x):
    rows = x.shape[0]
    moved = pltpu.roll(x, rows - 1, 0)
    return jnp.where(iota2(x.shape, 0) == rows - 1, 0.0, moved)


def merge(a, b):
    return jnp.concatenate([a[:, 0:128], a[:, 128:256] + b[:, 0:128], b[:, 128:256]], 1)


def group_of(lane):
    left = jnp.where(lane < 416, 2, 4)
    right = jnp.where(lane < 608, 5, 1)
    return jnp.where(lane < 384, lane // 96, jnp.where(lane < 512, left, right))


def channel_of(lane):
    left = jnp.where(lane < 416, lane - 384 + 64, lane - 416)
    right = jnp.where(lane < 608, lane - 512, lane - 608)
    return jnp.where(lane < 384, lane % 96, jnp.where(lane < 512, left, right))


def encoder_kernel(
    sizes,
    video_hbm, gain1_hbm, w1_hbm, wd_hbm, gain2_hbm, w2_hbm, shortcut_hbm,
    out,
    video, gain1, w1, wd, gain2, w2, shortcut,
    ones1, ones2, gain_lanes2,
    first, sides, resid, wa, wb, wda, wdb, acc_a, acc_b, section, part_out, part_in,
    z_out, z_in, yc_wide, yc_out, yc_in,
    tiles, windows, raw, wa2, wb2, wsa, wsb,
    near_send, near_recv, z_send, z_recv, yc_send, yc_recv, load,
):
    row_total, tm_total, clip_total, z_total = sizes
    y_total = row_total // z_total
    square = y_total * clip_total
    tm = lax.axis_index("tm")
    row = lax.axis_index("rows")
    clip = lax.axis_index("clip")
    z, y = row // y_total, row % y_total
    spot = y * clip_total + clip
    has_up, has_down = row > 0, row < row_total - 1
    has_past, has_next = tm > 0, tm < tm_total - 1
    up, down = (tm, row - 1, clip), (tm, row + 1, clip)
    past, after = (tm - 1, row, clip), (tm + 1, row, clip)

    def z_partner(step):
        other = (z + step) % z_total
        return other, (tm, other * y_total + y, clip)

    def square_partner(step):
        other = (spot + step) % square
        return other, (tm, z * y_total + other // clip_total, other % clip_total)

    barrier = pltpu.get_barrier_semaphore()
    for exists, who in ((has_up, up), (has_down, down), (has_past, past), (has_next, after)):
        @pl.when(exists)
        def _():
            pl.semaphore_signal(barrier, inc=1, device_id=who, device_id_type=MESH)
    for step in range(1, z_total):
        pl.semaphore_signal(barrier, inc=1, device_id=z_partner(step)[1], device_id_type=MESH)
    for step in range(1, square):
        pl.semaphore_signal(barrier, inc=1, device_id=square_partner(step)[1], device_id_type=MESH)

    loads = [
        pltpu.make_async_copy(src, dst, load.at[n])
        for n, (src, dst) in enumerate((
            (video_hbm, video), (gain1_hbm, gain1), (w1_hbm, w1), (wd_hbm, wd),
            (gain2_hbm, gain2), (w2_hbm, w2), (shortcut_hbm, shortcut)))]
    for one in loads:
        one.start()

    def remote(src, dst, index, who):
        return pltpu.make_async_remote_copy(
            src_ref=src, dst_ref=dst, send_sem=near_send.at[index], recv_sem=near_recv.at[index],
            device_id=who, device_id_type=MESH)

    ones1[...] = jnp.where(
        iota2((768, 384), 0) % 384 // 96 == iota2((768, 384), 1) // 96, 1.0, 0.0).astype(BF16)
    line = iota2((128, 128), 0)
    order = jnp.where(
        iota2((128, 128), 1) == jnp.where(line < 64, 2 * line, 2 * line - 127), 1.0, 0.0).astype(BF16)
    loads[1].wait()
    gain_lanes1 = 0.5 * place_exact(
        gain1[...], jnp.where(iota2((96, 384), 1) % 96 == iota2((96, 384), 0), 1.0, 0.0).astype(BF16))
    loads[0].wait()

    def norm_first(t):
        values = jnp.concatenate([dot(order, video[t, 0]), dot(order, video[t, 1])], 0)
        resid[t] = values.astype(BF16).reshape(2, 128, 384)
        meansq = dot(squares_split(values), ones1[...]) * (1.0 / 96.0)
        first[t + 2, 1:3] = normsilu(values, meansq, gain_lanes1).astype(BF16).reshape(2, 128, 384)

    norm_first(2)
    norm_first(3)

    count = has_up.astype(jnp.int32) + has_down.astype(jnp.int32) + has_past.astype(jnp.int32) + has_next.astype(jnp.int32)
    pl.semaphore_wait(barrier, count + (z_total - 1) + (square - 1))

    down_late = remote(first.at[4:6, 2], first.at[4:6, 0], 0, down)
    down_early = remote(first.at[2:4, 2], first.at[2:4, 0], 1, down)
    up_late = remote(first.at[4:6, 1], first.at[4:6, 3], 2, up)
    up_early = remote(first.at[2:4, 1], first.at[2:4, 3], 3, up)
    frames = remote(first.at[4:6, 1:3], first.at[0:2, 1:3], 4, after)
    corner_top = remote(first.at[4:6, 0], first.at[0:2, 0], 5, after)
    corner_low = remote(first.at[4:6, 3], first.at[0:2, 3], 6, after)
    partials = [remote(part_out.at[n], part_in.at[n], 7 + n, up) for n in range(2)]
    later = remote(windows.at[1, 4:6], windows.at[1, 0:2], 9, after)

    def when(condition, *steps):
        @pl.when(condition)
        def _():
            for step in steps:
                step()

    when(has_down, down_late.start)
    when(has_up, up_late.start)
    when(has_next, frames.start)
    norm_first(0)
    norm_first(1)
    when(has_down, down_early.start)
    when(has_up, up_early.start)

    @pl.when(jnp.logical_not(has_up))
    def _():
        first[:, 0] = jnp.zeros((6, 128, 384), BF16)

    @pl.when(jnp.logical_not(has_down))
    def _():
        first[:, 3] = jnp.zeros((6, 128, 384), BF16)
        part_in[...] = jnp.zeros((2, 2, 64, 384), BF16)

    @pl.when(jnp.logical_not(has_past))
    def _():
        first[0:2, 1:3] = jnp.zeros((2, 2, 128, 384), BF16)
        windows[1, 0:2] = jnp.zeros((2, 64, 640), BF16)

        @pl.when(has_up)
        def _():
            first[0:2, 0] = jnp.zeros((2, 128, 384), BF16)

        @pl.when(has_down)
        def _():
            first[0:2, 3] = jnp.zeros((2, 128, 384), BF16)

    lane = iota2((96, 1024), 1)
    offset = jnp.where(lane < 256, 0, jnp.where(lane < 512, 256 + 96, jnp.where(lane < 768, 512 + 64, 768 + 160)))
    places = jnp.where(lane == iota2((96, 1024), 0) + offset, 1.0, 0.0).astype(BF16)
    loads[2].wait()

    def weight_step(tap, carry):
        placed = dot(w1[tap], places)
        a0, a1 = placed[:, 0:256], placed[:, 256:512]
        b0, b1 = placed[:, 512:768], placed[:, 768:1024]
        spot = 3 * (tap % 3) + tap // 3
        wa[spot, 0:96] = (a0[96:192] + a1[0:96]).astype(BF16)
        wa[spot, 96:192] = (a0[192:288] + a1[96:192]).astype(BF16)
        wa[spot, 192:288] = a1[192:288].astype(BF16)
        wa[spot, 288:384] = a0[0:96].astype(BF16)
        wb[spot, 0:96] = b1[192:288].astype(BF16)
        wb[spot, 96:192] = b0[0:96].astype(BF16)
        wb[spot, 192:288] = (b0[96:192] + b1[0:96]).astype(BF16)
        wb[spot, 288:384] = (b0[192:288] + b1[96:192]).astype(BF16)
        return carry

    lax.fori_loop(0, 9, weight_step, 0)

    lane64 = iota2((64, 128), 1)

    def side_tiles(t, r):
        e0 = first[t, r, 0:64, 0:128].astype(F32)
        o0 = first[t, r, 64:128, 0:128].astype(F32)
        e2 = first[t, r, 0:64, 256:384].astype(F32)
        o2 = first[t, r, 64:128, 256:384].astype(F32)
        sides[0, t, r, 0:64] = jnp.where(lane64 < 32, e2, shift_down(o2)).astype(BF16)
        sides[0, t, r, 64:128] = jnp.where(lane64 < 32, o2, e2).astype(BF16)
        sides[1, t, r, 0:64] = jnp.where(lane64 < 96, o0, e0).astype(BF16)
        sides[1, t, r, 64:128] = jnp.where(lane64 < 96, shift_up(e0), o0).astype(BF16)

    def conv_part(r, taps, t):
        left, right = [], []
        for i in taps:
            for a in range(3):
                cells = slice(t + a, t + a + 2)
                left += [
                    first[cells, r + i, :, 0:256].reshape(256, 256),
                    sides[0, cells, r + i].reshape(256, 128)]
                right += [
                    sides[1, cells, r + i].reshape(256, 128),
                    first[cells, r + i, :, 128:384].reshape(256, 256)]
        lo, hi = 3 * taps[0], 3 * taps[-1] + 3
        deep = (hi - lo) * 384
        return (dot(jnp.concatenate(left, 1), wa[lo:hi].reshape(deep, 256)),
                dot(jnp.concatenate(right, 1), wb[lo:hi].reshape(deep, 256)))

    def conv_local(t):
        for r, taps in ((0, (1, 2)), (1, (0, 1))):
            part_a, part_b = conv_part(r, taps, t)
            acc_a[r, t:t + 2] = part_a.reshape(2, 128, 256)
            acc_b[r, t:t + 2] = part_b.reshape(2, 128, 256)

    def conv_finish(r, t):
        part_a, part_b = conv_part(r, (0,) if r == 0 else (2,), t)
        part_a += acc_a[r, t:t + 2].reshape(256, 256)
        part_b += acc_b[r, t:t + 2].reshape(256, 256)
        total = merge(part_a, part_b) + resid[t:t + 2, r].reshape(256, 384).astype(F32)
        section[t:t + 2, r] = total.astype(BF16).reshape(2, 128, 384)

    for t in (4, 5, 2, 3):
        for r in (1, 2):
            side_tiles(t, r)
    conv_local(2)

    def forward_top():
        down_late.wait_recv()
        when(has_next, corner_top.start)

    def forward_low():
        up_late.wait_recv()
        when(has_next, corner_low.start)

    when(has_up, forward_top)
    when(has_down, forward_low)

    loads[3].wait()

    def down_weight_step(tap, carry):
        placed = dot(wd[tap], places)
        for ref, base in ((wda, 0), (wdb, 512)):
            p0, p1 = placed[:, base:base + 256], placed[:, base + 256:base + 512]
            ref[tap, 0:96] = p0[0:96].astype(BF16)
            ref[tap, 96:192] = p0[96:192].astype(BF16)
            ref[tap, 192:288] = (p0[192:288] + p1[0:96]).astype(BF16)
            ref[tap, 288:384] = p1[96:192].astype(BF16)
            ref[tap, 384:480] = p1[192:288].astype(BF16)
            ref[tap, 480:512] = jnp.zeros((32, 256), BF16)
        return carry

    lax.fori_loop(0, 3, down_weight_step, 0)

    lane2 = iota2((192, 768), 1)
    source2 = iota2((192, 768), 0)
    places2 = jnp.where(lane2 == jnp.where(lane2 < 384, source2, source2 + 576), 1.0, 0.0).astype(BF16)
    loads[5].wait()

    def weight2_step(tap, carry):
        placed = dot(w2[tap], places2)
        p0, p1 = placed[:, 0:384], placed[:, 384:768]
        wa2[tap, 0:96] = (p0[96:192] + p1[0:96]).astype(BF16)
        wa2[tap, 96:192] = (p0[192:288] + p1[96:192]).astype(BF16)
        wa2[tap, 192:288] = p1[192:288].astype(BF16)
        wa2[tap, 288:384] = p0[0:96].astype(BF16)
        wb2[tap, 0:96] = p1[192:288].astype(BF16)
        wb2[tap, 96:192] = p0[0:96].astype(BF16)
        wb2[tap, 192:288] = (p0[96:192] + p1[0:96]).astype(BF16)
        wb2[tap, 288:384] = (p0[192:288] + p1[96:192]).astype(BF16)
        return carry

    lax.fori_loop(0, 9, weight2_step, 0)

    def halo_frames():
        frames.wait_recv()

    when(has_past, halo_frames)
    for t in (0, 1):
        for r in (1, 2):
            side_tiles(t, r)
    conv_local(0)

    loads[6].wait()
    placed2 = dot(shortcut[...], places2).astype(BF16)
    wsa[0:96] = placed2[:, 0:384]
    wsa[96:192] = placed2[:, 384:768]
    wsa[192:384] = jnp.zeros((192, 384), BF16)
    wsb[0:192] = jnp.zeros((192, 384), BF16)
    wsb[192:288] = placed2[:, 0:384]
    wsb[288:384] = placed2[:, 384:768]
    rows640 = iota2((640, 640), 0)
    twice = jnp.logical_or(jnp.logical_and(rows640 >= 384, rows640 < 416), rows640 >= 608)
    from_group = jnp.where(twice, -1, group_of(rows640))
    same = jnp.where(from_group == group_of(iota2((640, 640), 1)), 1.0, 0.0).astype(BF16)
    ones2[0:640] = same
    ones2[640:1280] = same
    loads[4].wait()
    gain_lanes2[...] = jnp.broadcast_to(0.5 * place_exact(gain2[...], jnp.where(
        channel_of(iota2((96, 640), 1)) == iota2((96, 640), 0), 1.0, 0.0).astype(BF16)), (8, 640))

    def down_rows(t, r):
        pieces = [], []
        for f in (t, t + 1):
            even = section[f, r, 0:64]
            odd = section[f, r, 64:128]
            following = shift_up(even[:, 0:128].astype(F32)).astype(BF16)
            pieces[0].append(jnp.concatenate([even, odd[:, 0:128]], 1))
            pieces[1].append(jnp.concatenate([odd, following], 1))
        return jnp.concatenate(pieces[0], 0), jnp.concatenate(pieces[1], 0)

    when(has_up, down_early.wait_recv)
    for half, t in ((0, 2), (1, 0)):
        if half == 0:
            frames_here = (4, 5, 2, 3)
        else:
            frames_here = (0, 1)

            @pl.when(jnp.logical_and(has_past, has_up))
            def _():
                corner_top.wait_recv()
        for f in frames_here:
            side_tiles(f, 0)
        conv_finish(0, t)
        left, right = down_rows(t, 0)
        part_out[half] = merge(dot(left, wda[2]), dot(right, wdb[2])).astype(BF16).reshape(2, 64, 384)
        when(has_up, partials[half].start)

    when(has_down, up_early.wait_recv)
    for f in (4, 5, 2, 3):
        side_tiles(f, 3)
    conv_finish(1, 2)

    def reduce_half(half, t):
        left0, right0 = down_rows(t, 0)
        left1, right1 = down_rows(t, 1)
        own = merge(dot(left0, wda[0]) + dot(left1, wda[1]), dot(right0, wdb[0]) + dot(right1, wdb[1]))
        when(has_down, partials[half].wait_recv)
        total = (own + part_in[half].reshape(128, 384).astype(F32)).astype(BF16).astype(F32)
        spot_in_block = iota2((64, 128), 0) % 8
        wide = []
        for f in range(2):
            cell = total[64 * f:64 * f + 64]
            edge = jnp.where(spot_in_block < 4, shift_down(cell[:, 256:384]), shift_up(cell[:, 0:128]))
            wide.append(jnp.concatenate([cell, edge], 1).reshape(z_total, 8, 512))
        z_out[half] = jnp.concatenate(wide, 1).astype(BF16)

    def z_copy(half, step, arriving):
        other, who = z_partner(step)
        here = (z - step + z_total) % z_total
        slot = half * z_total + step
        return pltpu.make_async_remote_copy(
            src_ref=z_out.at[half, other], dst_ref=z_in.at[half, here if arriving else z],
            send_sem=z_send.at[slot], recv_sem=z_recv.at[slot], device_id=who, device_id_type=MESH)

    def send_z(half):
        for step in range(1, z_total):
            z_copy(half, step, False).start()
        z_in[half, z] = z_out[half, z]

    reduce_half(0, 2)
    send_z(0)

    @pl.when(jnp.logical_and(has_past, has_down))
    def _():
        corner_low.wait_recv()
    for f in (0, 1):
        side_tiles(f, 3)
    conv_finish(1, 0)
    reduce_half(1, 0)
    send_z(1)

    def yc_copy(half, step, arriving):
        other, who = square_partner(step)
        here = (spot - step + square) % square
        slot = half * square + step
        return pltpu.make_async_remote_copy(
            src_ref=yc_out.at[half, other], dst_ref=yc_in.at[half, here if arriving else spot],
            send_sem=yc_send.at[slot], recv_sem=yc_recv.at[slot], device_id=who, device_id_type=MESH)

    lane8 = iota2((8, 128), 1)
    line8 = iota2((8, 128), 0)

    def relay(half):
        for step in range(1, z_total):
            z_copy(half, step, True).wait_recv()
        for source in range(z_total):
            cells = z_in[half, source].astype(F32)
            for f in range(2):
                cell = cells[8 * f:8 * f + 8]
                t0, t1, t2, edge = (cell[:, 128 * n:128 * n + 128] for n in range(4))
                before = jnp.where(line8 == 0, edge, pltpu.roll(t2, 1, 0))
                following = jnp.where(line8 == 7, edge, pltpu.roll(t0, 7, 0))
                parts = (t0, t1, t2, jnp.where(lane8 < 32, t2, before), jnp.where(lane8 < 96, following, t0))
                for n, part in enumerate(parts):
                    yc_wide[n, pl.ds(f * 8 + source, 8, stride=16), :] = part
        for n in range(5):
            yc_out[half, :, :, 128 * n:128 * n + 128] = yc_wide[n].astype(BF16).reshape(8, 16, 128)
        for step in range(1, square):
            yc_copy(half, step, False).start()
        yc_in[half, spot] = yc_out[half, spot]

    relay(0)
    relay(1)

    def norm_second(half, t):
        for step in range(1, square):
            yc_copy(half, step, True).wait_recv()
        for source in range(square):
            cells = yc_in[half, source].astype(F32)
            start = (source % clip_total) * row_total + source // clip_total
            for f in range(2):
                for n in range(5):
                    tiles[n, pl.ds(64 * f + start, 8, stride=y_total), :] = cells[8 * f:8 * f + 8, 128 * n:128 * n + 128]
        values = jnp.concatenate([tiles[n] for n in range(5)], 1)
        raw[t:t + 2] = values[:, 0:384].astype(BF16).reshape(2, 64, 384)
        meansq = dot(squares_split(values), ones2[...]) * (1.0 / 96.0)
        second = normsilu(values, meansq, gain_lanes2[0:1])
        windows[1, t + 2:t + 4] = second.astype(BF16).reshape(2, 64, 640)
        return second

    def shifted(second, t):
        line = iota2((128, 640), 0) % 32
        windows[0, t:t + 2] = jnp.where(line == 0, 0.0, pltpu.roll(second, 1, 0)).astype(BF16).reshape(2, 64, 640)
        windows[2, t:t + 2] = jnp.where(line == 31, 0.0, pltpu.roll(second, 127, 0)).astype(BF16).reshape(2, 64, 640)

    second = norm_second(0, 2)
    when(has_next, later.start)
    shifted(second, 4)
    second = norm_second(1, 0)
    shifted(second, 2)
    when(has_past, later.wait_recv)
    shifted(windows[1, 0:2].reshape(128, 640).astype(F32), 0)

    def conv(weights, direct, lane_sets):
        acc = dot(raw[...].reshape(256, 384), direct[...])
        for a in range(3):
            pieces = []
            for i in range(3):
                pieces += [windows[i, a:a + 4, :, lo:hi].reshape(256, hi - lo) for lo, hi in lane_sets]
            acc += dot(jnp.concatenate(pieces, 1), weights[3 * a:3 * a + 3].reshape(1152, 384))
        return acc.astype(BF16).reshape(4, 2, 32, 384)

    left = conv(wa2, wsa, ((0, 256), (384, 512)))
    for c in range(2):
        out[c, :, :, 0:384] = left[:, c]
    right = conv(wb2, wsb, ((512, 640), (128, 384)))
    for c in range(2):
        out[c, :, :, 384:768] = right[:, c]

    when(has_down, down_late.wait_send, down_early.wait_send)
    when(has_up, up_late.wait_send, up_early.wait_send, partials[0].wait_send, partials[1].wait_send)
    when(has_next, frames.wait_send, later.wait_send)

    @pl.when(jnp.logical_and(has_next, has_up))
    def _():
        corner_top.wait_send()

    @pl.when(jnp.logical_and(has_next, has_down))
    def _():
        corner_low.wait_send()

    for half in range(2):
        for step in range(1, z_total):
            z_copy(half, step, False).wait_send()
        for step in range(1, square):
            yc_copy(half, step, False).wait_send()


def vmem(shape, dtype=BF16):
    return pltpu.VMEM(shape, dtype)


def shards(sizes, video, gain_first, conv_first, down, gain_second, conv_second, shortcut):
    dma = pltpu.SemaphoreType.DMA
    latents = pl.pallas_call(
        functools.partial(encoder_kernel, sizes),
        out_shape=jax.ShapeDtypeStruct((2, 4, 32, 768), BF16),
        in_specs=[pl.BlockSpec(memory_space=pl.ANY)] * 7,
        out_specs=pl.BlockSpec(memory_space=pltpu.VMEM),
        scratch_shapes=[
            vmem((4, 2, 128, 384)), vmem((1, 96), F32), vmem((9, 288, 96)), vmem((3, 288, 96)),
            vmem((1, 96), F32), vmem((9, 288, 192)), vmem((96, 192)),
            vmem((768, 384)), vmem((1280, 640)), vmem((8, 640), F32),
            vmem((6, 4, 128, 384)), vmem((2, 6, 4, 128, 128)), vmem((4, 2, 128, 384)),
            vmem((9, 384, 256)), vmem((9, 384, 256)), vmem((3, 512, 256)), vmem((3, 512, 256)),
            vmem((2, 4, 128, 256), F32), vmem((2, 4, 128, 256), F32),
            vmem((4, 2, 128, 384)),
            vmem((2, 2, 64, 384)), vmem((2, 2, 64, 384)),
            vmem((2, 8, 16, 512)), vmem((2, 8, 16, 512)),
            vmem((5, 128, 128), F32), vmem((2, 8, 16, 640)), vmem((2, 8, 16, 640)),
            vmem((5, 128, 128), F32), vmem((3, 6, 64, 640)), vmem((4, 64, 384)),
            vmem((9, 384, 384)), vmem((9, 384, 384)), vmem((384, 384)), vmem((384, 384)),
            dma((10,)), dma((10,)), dma((16,)), dma((16,)), dma((16,)), dma((16,)), dma((7,)),
        ],
        compiler_params=pltpu.CompilerParams(
            collective_id=0, has_side_effects=True, vmem_limit_bytes=VMEM_LIMIT),
        name="encoder",
    )(
        video.reshape(4, 2, 128, 384), gain_first.reshape(1, 96),
        conv_first.reshape(9, 288, 96), down.reshape(3, 288, 96),
        gain_second.reshape(1, 96), conv_second.reshape(9, 288, 192), shortcut,
    )
    return latents.reshape(2, 4, 32, 1, 768)


def solution(mesh):
    sizes = (mesh.shape["rows"], mesh.shape["tm"], mesh.shape["clip"], 8)
    return jax.shard_map(
        functools.partial(shards, sizes),
        mesh=mesh,
        in_specs=(P("clip", "tm", "rows", None, None), P(), P(), P(), P(), P(), P()),
        out_specs=P(None, "tm", None, ("rows", "clip"), None),
        check_vma=False,
    )
```

profile of v0, /device:TPU:1, one launch (start us, length us, event | category | flops | bytes accessed | tf_op | source)
XLA Modules:
  0.0 47.4 jit_solution(17949258436948196)
XLA Ops:
  0.0 45.6 %encoder.1 = bf16[2,4,32,768]{3,2,1,0:T(8,128)(2,1)} custom-call(bf16[4,2,128,384]{3,2,1,0:T(8,128)(2,1)} %bitcast.11, f32[1,96]{1,0:T(1,128)} %bitcast.14, bf16[9,288,96]{2,1,0:T(8,128)(2,1)} %bitcast.12, bf16[3,288,96]{2,1,0:T(8,128)(2,1)} %bitcast.13, f32[1,96]{1,0:T(1,128)} %bitcast.15, bf16[9,288,192]{2,1,0:T(8,128)(2,1)} %bitcast.10, ...), custom_call_target="tpu_custom_call" | custom-call | tf_op jit(solution)/shard_map/encoder/pallas_call | solution.py:515
  45.6 1.8 %copy.10 = bf16[2,4,32,1,768]{4,2,3,1,0:T(8,128)(2,1)} copy(bf16[2,4,32,1,768]{4,2,3,1,0:T(8,128)(2,1)} %bitcast.9) | data formatting | bytes 786432
where the time goes:
time: 47.5 us; the launch traced here: 47.4 us
  Pallas kernels  45.6 us (96%)
  local copies, waits for them, and re-layouts  1.77 us (4%)
    pallas_call x1, Pallas kernels, shards(): pl.pallas_call(functools.partial(encoder_kernel, sizes), out_shape=jax.Sh...  45.6 us
    unnamed x1, local copies, waits for them, and re-layouts  1.77 us

commit v1 on v0

--- a/solution.py
+++ b/solution.py
@@ -57,8 +57,12 @@
     return jnp.where(iota2(x.shape, 0) == rows - 1, 0.0, moved)
 
 
-def merge(a, b):
-    return jnp.concatenate([a[:, 0:128], a[:, 128:256] + b[:, 0:128], b[:, 128:256]], 1)
+def packed(cells):
+    c0, c1, c2, c3 = cells
+    lane = iota2(c0.shape, 1)
+    c1, c2, c3 = pltpu.roll(c1, 96, 1), pltpu.roll(c2, 64, 1), pltpu.roll(c3, 32, 1)
+    return jnp.concatenate(
+        [jnp.where(lane < 96, c0, c1), jnp.where(lane < 64, c1, c2), jnp.where(lane < 32, c2, c3)], 1)
 
 
 def group_of(lane):
@@ -79,7 +83,7 @@
     out,
     video, gain1, w1, wd, gain2, w2, shortcut,
     ones1, ones2, gain_lanes2,
-    first, sides, resid, wa, wb, wda, wdb, acc_a, acc_b, section, part_out, part_in,
+    first, cells1, cellsv, wdp, products, w5, part_out, part_in, own_sum,
     z_out, z_in, yc_wide, yc_out, yc_in,
     tiles, windows, raw, wa2, wb2, wsa, wsb,
     near_send, near_recv, z_send, z_recv, yc_send, yc_recv, load,
@@ -138,11 +142,33 @@
         gain1[...], jnp.where(iota2((96, 384), 1) % 96 == iota2((96, 384), 0), 1.0, 0.0).astype(BF16))
     loads[0].wait()
 
+    lane64 = iota2((64, 128), 1)
+    line64 = iota2((64, 128), 0)
+
+    def windows_of(even, odd):
+        return shift_up(even[:, 0:128]), shift_up(even[:, 128:256]), shift_down(odd[:, 256:384])
+
+    def spread_first(t, r, even, odd):
+        after0, after1, before2 = windows_of(even, odd)
+        last = jnp.where(line64 == 63, pltpu.roll(odd[:, 256:384], 32, 1), 0.0)
+        cells1[t, r, 0] = jnp.concatenate([
+            even, odd[:, 0:128], jnp.where(lane64 < 64, odd[:, 128:256], 0.0),
+            jnp.where(lane64 < 32, 0.0, before2)], 1).astype(BF16)
+        cells1[t, r, 1] = jnp.concatenate([
+            odd, after0, jnp.where(lane64 < 64, after1, last),
+            jnp.where(lane64 < 32, last, even[:, 256:384])], 1).astype(BF16)
+
     def norm_first(t):
         values = jnp.concatenate([dot(order, video[t, 0]), dot(order, video[t, 1])], 0)
-        resid[t] = values.astype(BF16).reshape(2, 128, 384)
         meansq = dot(squares_split(values), ones1[...]) * (1.0 / 96.0)
-        first[t + 2, 1:3] = normsilu(values, meansq, gain_lanes1).astype(BF16).reshape(2, 128, 384)
+        result = normsilu(values, meansq, gain_lanes1)
+        first[t + 2] = result.astype(BF16).reshape(2, 128, 384)
+        for r in range(2):
+            even, odd = values[128 * r:128 * r + 64], values[128 * r + 64:128 * r + 128]
+            cellsv[t, r, 0] = jnp.concatenate([even, odd[:, 0:128]], 1).astype(BF16)
+            cellsv[t, r, 1] = jnp.concatenate([odd, shift_up(even[:, 0:128])], 1).astype(BF16)
+            even, odd = result[128 * r:128 * r + 64], result[128 * r + 64:128 * r + 128]
+            spread_first(t + 2, r, even, odd)
 
     norm_first(2)
     norm_first(3)
@@ -150,15 +176,10 @@
     count = has_up.astype(jnp.int32) + has_down.astype(jnp.int32) + has_past.astype(jnp.int32) + has_next.astype(jnp.int32)
     pl.semaphore_wait(barrier, count + (z_total - 1) + (square - 1))
 
-    down_late = remote(first.at[4:6, 2], first.at[4:6, 0], 0, down)
-    down_early = remote(first.at[2:4, 2], first.at[2:4, 0], 1, down)
-    up_late = remote(first.at[4:6, 1], first.at[4:6, 3], 2, up)
-    up_early = remote(first.at[2:4, 1], first.at[2:4, 3], 3, up)
-    frames = remote(first.at[4:6, 1:3], first.at[0:2, 1:3], 4, after)
-    corner_top = remote(first.at[4:6, 0], first.at[0:2, 0], 5, after)
-    corner_low = remote(first.at[4:6, 3], first.at[0:2, 3], 6, after)
-    partials = [remote(part_out.at[n], part_in.at[n], 7 + n, up) for n in range(2)]
-    later = remote(windows.at[1, 4:6], windows.at[1, 0:2], 9, after)
+    frames = remote(first.at[4:6], first.at[0:2], 0, after)
+    ups = [remote(part_out.at[0, n], part_in.at[0, n], 1 + n, up) for n in range(2)]
+    downs = [remote(part_out.at[1, n], part_in.at[1, n], 3 + n, down) for n in range(2)]
+    later = remote(windows.at[1, 4:6], windows.at[1, 0:2], 5, after)
 
     def when(condition, *steps):
         @pl.when(condition)
@@ -166,130 +187,111 @@
             for step in steps:
                 step()
 
-    when(has_down, down_late.start)
-    when(has_up, up_late.start)
     when(has_next, frames.start)
     norm_first(0)
     norm_first(1)
-    when(has_down, down_early.start)
-    when(has_up, up_early.start)
 
     @pl.when(jnp.logical_not(has_up))
     def _():
-        first[:, 0] = jnp.zeros((6, 128, 384), BF16)
+        part_in[1] = jnp.zeros((2, 128, 384), BF16)
 
     @pl.when(jnp.logical_not(has_down))
     def _():
-        first[:, 3] = jnp.zeros((6, 128, 384), BF16)
-        part_in[...] = jnp.zeros((2, 2, 64, 384), BF16)
+        part_in[0] = jnp.zeros((2, 128, 384), BF16)
 
     @pl.when(jnp.logical_not(has_past))
     def _():
-        first[0:2, 1:3] = jnp.zeros((2, 2, 128, 384), BF16)
+        first[0:2] = jnp.zeros((2, 2, 128, 384), BF16)
         windows[1, 0:2] = jnp.zeros((2, 64, 640), BF16)
 
-        @pl.when(has_up)
-        def _():
-            first[0:2, 0] = jnp.zeros((2, 128, 384), BF16)
-
-        @pl.when(has_down)
-        def _():
-            first[0:2, 3] = jnp.zeros((2, 128, 384), BF16)
-
-    lane = iota2((96, 1024), 1)
-    offset = jnp.where(lane < 256, 0, jnp.where(lane < 512, 256 + 96, jnp.where(lane < 768, 512 + 64, 768 + 160)))
-    places = jnp.where(lane == iota2((96, 1024), 0) + offset, 1.0, 0.0).astype(BF16)
+    loads[3].wait()
+    wdp[...] = jnp.zeros((96, 1152), BF16)
+    for i in range(3):
+        for j in range(3):
+            wdp[:, 128 * (3 * i + j):128 * (3 * i + j) + 96] = wd[i, 96 * j:96 * j + 96]
+    blank = jnp.zeros((96, 128), F32)
+
+    def down_tap(i, j):
+        return wdp[:, 128 * (3 * i + j):128 * (3 * i + j) + 128]
+
+    for r, i in ((1, 0), (2, 1), (3, 2)):
+        none = blank.astype(BF16)
+        for n, (q0, q1) in enumerate((
+                (down_tap(i, 0), none), (down_tap(i, 1), none), (down_tap(i, 2), down_tap(i, 0)),
+                (none, down_tap(i, 1)), (none, down_tap(i, 2)))):
+            w5[r, 2304 + 96 * n:2400 + 96 * n] = jnp.concatenate([q0, q1], 1)
+        w5[r, 2784:2816] = jnp.zeros((32, 256), BF16)
+    below = has_down.astype(F32)
     loads[2].wait()
 
-    def weight_step(tap, carry):
-        placed = dot(w1[tap], places)
-        a0, a1 = placed[:, 0:256], placed[:, 256:512]
-        b0, b1 = placed[:, 512:768], placed[:, 768:1024]
-        spot = 3 * (tap % 3) + tap // 3
-        wa[spot, 0:96] = (a0[96:192] + a1[0:96]).astype(BF16)
-        wa[spot, 96:192] = (a0[192:288] + a1[96:192]).astype(BF16)
-        wa[spot, 192:288] = a1[192:288].astype(BF16)
-        wa[spot, 288:384] = a0[0:96].astype(BF16)
-        wb[spot, 0:96] = b1[192:288].astype(BF16)
-        wb[spot, 96:192] = b0[0:96].astype(BF16)
-        wb[spot, 192:288] = (b0[96:192] + b1[0:96]).astype(BF16)
-        wb[spot, 288:384] = (b0[192:288] + b1[96:192]).astype(BF16)
+    def compose_step(a, carry):
+        for i in range(3):
+            products[i] = dot(w1[3 * a + i], wdp[...])
+
+        def total(r, pairs):
+            result = None
+            for i in range(3):
+                lower = r - i
+                if 0 <= lower <= 2:
+                    for j, across in pairs:
+                        lane = 128 * (3 * lower + across)
+                        term = products[i, 96 * j:96 * j + 96, lane:lane + 128]
+                        if r == 2 and lower == 2:
+                            term = term * below
+                        result = term if result is None else result + term
+            return result
+
+        start = pl.multiple_of(a * 768, 128)
+        for r in range(5):
+            at = [total(r, [(j, c - j) for j in range(3) if 0 <= c - j <= 2]) for c in range(5)]
+            beyond = -total(r, [(0, 2)])
+            for n, (q0, q1) in enumerate((
+                    (at[1], blank), (at[2], at[0]), (at[3], at[1]), (at[4], at[2]),
+                    (blank, at[3]), (blank, at[4]), (blank, beyond), (at[0], blank))):
+                w5[r, pl.ds(start + 96 * n, 96)] = jnp.concatenate([q0, q1], 1).astype(BF16)
         return carry
 
-    lax.fori_loop(0, 9, weight_step, 0)
-
-    lane64 = iota2((64, 128), 1)
-
-    def side_tiles(t, r):
-        e0 = first[t, r, 0:64, 0:128].astype(F32)
-        o0 = first[t, r, 64:128, 0:128].astype(F32)
-        e2 = first[t, r, 0:64, 256:384].astype(F32)
-        o2 = first[t, r, 64:128, 256:384].astype(F32)
-        sides[0, t, r, 0:64] = jnp.where(lane64 < 32, e2, shift_down(o2)).astype(BF16)
-        sides[0, t, r, 64:128] = jnp.where(lane64 < 32, o2, e2).astype(BF16)
-        sides[1, t, r, 0:64] = jnp.where(lane64 < 96, o0, e0).astype(BF16)
-        sides[1, t, r, 64:128] = jnp.where(lane64 < 96, shift_up(e0), o0).astype(BF16)
-
-    def conv_part(r, taps, t):
-        left, right = [], []
-        for i in taps:
-            for a in range(3):
-                cells = slice(t + a, t + a + 2)
-                left += [
-                    first[cells, r + i, :, 0:256].reshape(256, 256),
-                    sides[0, cells, r + i].reshape(256, 128)]
-                right += [
-                    sides[1, cells, r + i].reshape(256, 128),
-                    first[cells, r + i, :, 128:384].reshape(256, 256)]
-        lo, hi = 3 * taps[0], 3 * taps[-1] + 3
-        deep = (hi - lo) * 384
-        return (dot(jnp.concatenate(left, 1), wa[lo:hi].reshape(deep, 256)),
-                dot(jnp.concatenate(right, 1), wb[lo:hi].reshape(deep, 256)))
-
-    def conv_local(t):
-        for r, taps in ((0, (1, 2)), (1, (0, 1))):
-            part_a, part_b = conv_part(r, taps, t)
-            acc_a[r, t:t + 2] = part_a.reshape(2, 128, 256)
-            acc_b[r, t:t + 2] = part_b.reshape(2, 128, 256)
-
-    def conv_finish(r, t):
-        part_a, part_b = conv_part(r, (0,) if r == 0 else (2,), t)
-        part_a += acc_a[r, t:t + 2].reshape(256, 256)
-        part_b += acc_b[r, t:t + 2].reshape(256, 256)
-        total = merge(part_a, part_b) + resid[t:t + 2, r].reshape(256, 384).astype(F32)
-        section[t:t + 2, r] = total.astype(BF16).reshape(2, 128, 384)
-
-    for t in (4, 5, 2, 3):
-        for r in (1, 2):
-            side_tiles(t, r)
-    conv_local(2)
-
-    def forward_top():
-        down_late.wait_recv()
-        when(has_next, corner_top.start)
-
-    def forward_low():
-        up_late.wait_recv()
-        when(has_next, corner_low.start)
-
-    when(has_up, forward_top)
-    when(has_down, forward_low)
-
-    loads[3].wait()
-
-    def down_weight_step(tap, carry):
-        placed = dot(wd[tap], places)
-        for ref, base in ((wda, 0), (wdb, 512)):
-            p0, p1 = placed[:, base:base + 256], placed[:, base + 256:base + 512]
-            ref[tap, 0:96] = p0[0:96].astype(BF16)
-            ref[tap, 96:192] = p0[96:192].astype(BF16)
-            ref[tap, 192:288] = (p0[192:288] + p1[0:96]).astype(BF16)
-            ref[tap, 288:384] = p1[96:192].astype(BF16)
-            ref[tap, 384:480] = p1[192:288].astype(BF16)
-            ref[tap, 480:512] = jnp.zeros((32, 256), BF16)
-        return carry
-
-    lax.fori_loop(0, 3, down_weight_step, 0)
+    lax.fori_loop(0, 3, compose_step, 0)
+
+    def row_cells(t, r, with_video):
+        pieces = [cells1[t + a:t + a + 2, r].reshape(256, 768) for a in range(3)]
+        if with_video:
+            pieces.append(cellsv[t:t + 2, r].reshape(256, 512))
+        return jnp.concatenate(pieces, 1)
+
+    def compact(total):
+        frames_here = []
+        for f in range(2):
+            base = 128 * f
+            frames_here.append(packed([
+                total[base + 64 * p:base + 64 * p + 64, 128 * q:128 * q + 128]
+                for p in range(2) for q in range(2)]))
+        return jnp.concatenate(frames_here, 0)
+
+    def send_partials(half, t):
+        total = dot(row_cells(t, 0, True), w5[3]) + dot(row_cells(t, 1, False), w5[4, 0:2304])
+        part_out[0, half] = compact(total).astype(BF16)
+        when(has_up, ups[half].start)
+        part_out[1, half] = compact(dot(row_cells(t, 1, False), w5[0, 0:2304])).astype(BF16)
+        when(has_down, downs[half].start)
+
+    def sum_own(half, t):
+        total = dot(row_cells(t, 0, True), w5[1]) + dot(row_cells(t, 1, True), w5[2])
+        own_sum[half] = compact(total)
+
+    send_partials(0, 2)
+
+    def halo_frames():
+        frames.wait_recv()
+
+    when(has_past, halo_frames)
+    for t in range(2):
+        for r in range(2):
+            cell = first[t, r].astype(F32)
+            spread_first(t, r, cell[0:64], cell[64:128])
+    send_partials(1, 0)
+    sum_own(0, 2)
+    sum_own(1, 0)
 
     lane2 = iota2((192, 768), 1)
     source2 = iota2((192, 768), 0)
@@ -310,15 +312,6 @@
         return carry
 
     lax.fori_loop(0, 9, weight2_step, 0)
-
-    def halo_frames():
-        frames.wait_recv()
-
-    when(has_past, halo_frames)
-    for t in (0, 1):
-        for r in (1, 2):
-            side_tiles(t, r)
-    conv_local(0)
 
     loads[6].wait()
     placed2 = dot(shortcut[...], places2).astype(BF16)
@@ -338,44 +331,11 @@
     gain_lanes2[...] = jnp.broadcast_to(0.5 * place_exact(gain2[...], jnp.where(
         channel_of(iota2((96, 640), 1)) == iota2((96, 640), 0), 1.0, 0.0).astype(BF16)), (8, 640))
 
-    def down_rows(t, r):
-        pieces = [], []
-        for f in (t, t + 1):
-            even = section[f, r, 0:64]
-            odd = section[f, r, 64:128]
-            following = shift_up(even[:, 0:128].astype(F32)).astype(BF16)
-            pieces[0].append(jnp.concatenate([even, odd[:, 0:128]], 1))
-            pieces[1].append(jnp.concatenate([odd, following], 1))
-        return jnp.concatenate(pieces[0], 0), jnp.concatenate(pieces[1], 0)
-
-    when(has_up, down_early.wait_recv)
-    for half, t in ((0, 2), (1, 0)):
-        if half == 0:
-            frames_here = (4, 5, 2, 3)
-        else:
-            frames_here = (0, 1)
-
-            @pl.when(jnp.logical_and(has_past, has_up))
-            def _():
-                corner_top.wait_recv()
-        for f in frames_here:
-            side_tiles(f, 0)
-        conv_finish(0, t)
-        left, right = down_rows(t, 0)
-        part_out[half] = merge(dot(left, wda[2]), dot(right, wdb[2])).astype(BF16).reshape(2, 64, 384)
-        when(has_up, partials[half].start)
-
-    when(has_down, up_early.wait_recv)
-    for f in (4, 5, 2, 3):
-        side_tiles(f, 3)
-    conv_finish(1, 2)
-
-    def reduce_half(half, t):
-        left0, right0 = down_rows(t, 0)
-        left1, right1 = down_rows(t, 1)
-        own = merge(dot(left0, wda[0]) + dot(left1, wda[1]), dot(right0, wdb[0]) + dot(right1, wdb[1]))
-        when(has_down, partials[half].wait_recv)
-        total = (own + part_in[half].reshape(128, 384).astype(F32)).astype(BF16).astype(F32)
+    def reduce_half(half):
+        when(has_down, ups[half].wait_recv)
+        when(has_up, downs[half].wait_recv)
+        total = own_sum[half] + part_in[0, half].astype(F32) + part_in[1, half].astype(F32)
+        total = total.astype(BF16).astype(F32)
         spot_in_block = iota2((64, 128), 0) % 8
         wide = []
         for f in range(2):
@@ -397,16 +357,9 @@
             z_copy(half, step, False).start()
         z_in[half, z] = z_out[half, z]
 
-    reduce_half(0, 2)
+    reduce_half(0)
     send_z(0)
-
-    @pl.when(jnp.logical_and(has_past, has_down))
-    def _():
-        corner_low.wait_recv()
-    for f in (0, 1):
-        side_tiles(f, 3)
-    conv_finish(1, 0)
-    reduce_half(1, 0)
+    reduce_half(1)
     send_z(1)
 
     def yc_copy(half, step, arriving):
@@ -487,18 +440,9 @@
     for c in range(2):
         out[c, :, :, 384:768] = right[:, c]
 
-    when(has_down, down_late.wait_send, down_early.wait_send)
-    when(has_up, up_late.wait_send, up_early.wait_send, partials[0].wait_send, partials[1].wait_send)
+    when(has_up, ups[0].wait_send, ups[1].wait_send)
+    when(has_down, downs[0].wait_send, downs[1].wait_send)
     when(has_next, frames.wait_send, later.wait_send)
-
-    @pl.when(jnp.logical_and(has_next, has_up))
-    def _():
-        corner_top.wait_send()
-
-    @pl.when(jnp.logical_and(has_next, has_down))
-    def _():
-        corner_low.wait_send()
-
     for half in range(2):
         for step in range(1, z_total):
             z_copy(half, step, False).wait_send()
@@ -521,16 +465,14 @@
             vmem((4, 2, 128, 384)), vmem((1, 96), F32), vmem((9, 288, 96)), vmem((3, 288, 96)),
             vmem((1, 96), F32), vmem((9, 288, 192)), vmem((96, 192)),
             vmem((768, 384)), vmem((1280, 640)), vmem((8, 640), F32),
-            vmem((6, 4, 128, 384)), vmem((2, 6, 4, 128, 128)), vmem((4, 2, 128, 384)),
-            vmem((9, 384, 256)), vmem((9, 384, 256)), vmem((3, 512, 256)), vmem((3, 512, 256)),
-            vmem((2, 4, 128, 256), F32), vmem((2, 4, 128, 256), F32),
-            vmem((4, 2, 128, 384)),
-            vmem((2, 2, 64, 384)), vmem((2, 2, 64, 384)),
+            vmem((6, 2, 128, 384)), vmem((6, 2, 2, 64, 768)), vmem((4, 2, 2, 64, 512)),
+            vmem((96, 1152)), vmem((3, 288, 1152), F32), vmem((5, 2816, 256)),
+            vmem((2, 2, 128, 384)), vmem((2, 2, 128, 384)), vmem((2, 128, 384), F32),
             vmem((2, 8, 16, 512)), vmem((2, 8, 16, 512)),
             vmem((5, 128, 128), F32), vmem((2, 8, 16, 640)), vmem((2, 8, 16, 640)),
             vmem((5, 128, 128), F32), vmem((3, 6, 64, 640)), vmem((4, 64, 384)),
             vmem((9, 384, 384)), vmem((9, 384, 384)), vmem((384, 384)), vmem((384, 384)),
-            dma((10,)), dma((10,)), dma((16,)), dma((16,)), dma((16,)), dma((16,)), dma((7,)),
+            dma((6,)), dma((6,)), dma((16,)), dma((16,)), dma((16,)), dma((16,)), dma((7,)),
         ],
         compiler_params=pltpu.CompilerParams(
             collective_id=0, has_side_effects=True, vmem_limit_bytes=VMEM_LIMIT),

time: 47.5 us -> 41.4 us (0.87)
  Pallas kernels: 45.6 us -> 39.5 us
    pallas_call x1, Pallas kernels: 45.6 us -> 39.5 us  [shards(): pl.pallas_call(functools.partial(encoder_kernel, sizes), out_shape=jax.Sh...]
where the time goes in v1:
time: 41.4 us; the launch traced here: 41.3 us
  Pallas kernels  39.5 us (95%)
  local copies, waits for them, and re-layouts  1.77 us (4%)
    pallas_call x1, Pallas kernels, shards(): pl.pallas_call(functools.partial(encoder_kernel, sizes), out_shape=jax.Sh...  39.5 us
    unnamed x1, local copies, waits for them, and re-layouts  1.77 us

profile of v1, /device:TPU:1, one launch (start us, length us, event | category | flops | bytes accessed | tf_op | source)
XLA Modules:
  0.0 41.3 jit_solution(13502513575571620896)
XLA Ops:
  0.0 39.5 %encoder.1 = bf16[2,4,32,768]{3,2,1,0:T(8,128)(2,1)} custom-call(bf16[4,2,128,384]{3,2,1,0:T(8,128)(2,1)} %bitcast.11, f32[1,96]{1,0:T(1,128)} %bitcast.14, bf16[9,288,96]{2,1,0:T(8,128)(2,1)} %bitcast.12, bf16[3,288,96]{2,1,0:T(8,128)(2,1)} %bitcast.13, f32[1,96]{1,0:T(1,128)} %bitcast.15, bf16[9,288,192]{2,1,0:T(8,128)(2,1)} %bitcast.10, ...), custom_call_target="tpu_custom_call" | custom-call | tf_op jit(solution)/shard_map/encoder/pallas_call | solution.py:459
  39.5 1.8 %copy.10 = bf16[2,4,32,1,768]{4,2,3,1,0:T(8,128)(2,1)} copy(bf16[2,4,32,1,768]{4,2,3,1,0:T(8,128)(2,1)} %bitcast.9) | data formatting | bytes 786432

commit v2 on v1

--- a/solution.py
+++ b/solution.py
@@ -83,7 +83,7 @@
     out,
     video, gain1, w1, wd, gain2, w2, shortcut,
     ones1, ones2, gain_lanes2,
-    first, cells1, cellsv, wdp, products, w5, part_out, part_in, own_sum,
+    past_video, cells1, cellsv, wdp, products, w5, part_out, part_in, own_sum,
     z_out, z_in, yc_wide, yc_out, yc_in,
     tiles, windows, raw, wa2, wb2, wsa, wsb,
     near_send, near_recv, z_send, z_recv, yc_send, yc_recv, load,
@@ -132,6 +132,17 @@
             src_ref=src, dst_ref=dst, send_sem=near_send.at[index], recv_sem=near_recv.at[index],
             device_id=who, device_id_type=MESH)
 
+    frames = remote(video_hbm.at[2:4], past_video, 0, after)
+    ups = [remote(part_out.at[0, n], part_in.at[0, n], 1 + n, up) for n in range(2)]
+    downs = [remote(part_out.at[1, n], part_in.at[1, n], 3 + n, down) for n in range(2)]
+    later = remote(windows.at[1, 4:6], windows.at[1, 0:2], 5, after)
+
+    def when(condition, *steps):
+        @pl.when(condition)
+        def _():
+            for step in steps:
+                step()
+
     ones1[...] = jnp.where(
         iota2((768, 384), 0) % 384 // 96 == iota2((768, 384), 1) // 96, 1.0, 0.0).astype(BF16)
     line = iota2((128, 128), 0)
@@ -158,38 +169,28 @@
             odd, after0, jnp.where(lane64 < 64, after1, last),
             jnp.where(lane64 < 32, last, even[:, 256:384])], 1).astype(BF16)
 
-    def norm_first(t):
-        values = jnp.concatenate([dot(order, video[t, 0]), dot(order, video[t, 1])], 0)
+    def norm_first(t, source, f):
+        values = jnp.concatenate([dot(order, source[f, 0]), dot(order, source[f, 1])], 0)
         meansq = dot(squares_split(values), ones1[...]) * (1.0 / 96.0)
         result = normsilu(values, meansq, gain_lanes1)
-        first[t + 2] = result.astype(BF16).reshape(2, 128, 384)
+        for r in range(2):
+            even, odd = result[128 * r:128 * r + 64], result[128 * r + 64:128 * r + 128]
+            spread_first(t, r, even, odd)
+        return values
+
+    def norm_own(t):
+        values = norm_first(t + 2, video, t)
         for r in range(2):
             even, odd = values[128 * r:128 * r + 64], values[128 * r + 64:128 * r + 128]
             cellsv[t, r, 0] = jnp.concatenate([even, odd[:, 0:128]], 1).astype(BF16)
             cellsv[t, r, 1] = jnp.concatenate([odd, shift_up(even[:, 0:128])], 1).astype(BF16)
-            even, odd = result[128 * r:128 * r + 64], result[128 * r + 64:128 * r + 128]
-            spread_first(t + 2, r, even, odd)
-
-    norm_first(2)
-    norm_first(3)
+
+    for t in range(4):
+        norm_own(t)
 
     count = has_up.astype(jnp.int32) + has_down.astype(jnp.int32) + has_past.astype(jnp.int32) + has_next.astype(jnp.int32)
     pl.semaphore_wait(barrier, count + (z_total - 1) + (square - 1))
-
-    frames = remote(first.at[4:6], first.at[0:2], 0, after)
-    ups = [remote(part_out.at[0, n], part_in.at[0, n], 1 + n, up) for n in range(2)]
-    downs = [remote(part_out.at[1, n], part_in.at[1, n], 3 + n, down) for n in range(2)]
-    later = remote(windows.at[1, 4:6], windows.at[1, 0:2], 5, after)
-
-    def when(condition, *steps):
-        @pl.when(condition)
-        def _():
-            for step in steps:
-                step()
-
     when(has_next, frames.start)
-    norm_first(0)
-    norm_first(1)
 
     @pl.when(jnp.logical_not(has_up))
     def _():
@@ -201,7 +202,7 @@
 
     @pl.when(jnp.logical_not(has_past))
     def _():
-        first[0:2] = jnp.zeros((2, 2, 128, 384), BF16)
+        past_video[...] = jnp.zeros((2, 2, 128, 384), BF16)
         windows[1, 0:2] = jnp.zeros((2, 64, 640), BF16)
 
     loads[3].wait()
@@ -279,18 +280,44 @@
         total = dot(row_cells(t, 0, True), w5[1]) + dot(row_cells(t, 1, True), w5[2])
         own_sum[half] = compact(total)
 
+    def reduce_half(half):
+        when(has_down, ups[half].wait_recv)
+        when(has_up, downs[half].wait_recv)
+        total = own_sum[half] + part_in[0, half].astype(F32) + part_in[1, half].astype(F32)
+        total = total.astype(BF16).astype(F32)
+        spot_in_block = iota2((64, 128), 0) % 8
+        wide = []
+        for f in range(2):
+            cell = total[64 * f:64 * f + 64]
+            edge = jnp.where(spot_in_block < 4, shift_down(cell[:, 256:384]), shift_up(cell[:, 0:128]))
+            wide.append(jnp.concatenate([cell, edge], 1).reshape(z_total, 8, 512))
+        z_out[half] = jnp.concatenate(wide, 1).astype(BF16)
+
+    def z_copy(half, step, arriving):
+        other, who = z_partner(step)
+        here = (z - step + z_total) % z_total
+        slot = half * z_total + step
+        return pltpu.make_async_remote_copy(
+            src_ref=z_out.at[half, other], dst_ref=z_in.at[half, here if arriving else z],
+            send_sem=z_send.at[slot], recv_sem=z_recv.at[slot], device_id=who, device_id_type=MESH)
+
+    def send_z(half):
+        for step in range(1, z_total):
+            z_copy(half, step, False).start()
+        z_in[half, z] = z_out[half, z]
+
     send_partials(0, 2)
+    sum_own(0, 2)
 
     def halo_frames():
         frames.wait_recv()
 
     when(has_past, halo_frames)
     for t in range(2):
-        for r in range(2):
-            cell = first[t, r].astype(F32)
-            spread_first(t, r, cell[0:64], cell[64:128])
+        norm_first(t, past_video, t)
     send_partials(1, 0)
-    sum_own(0, 2)
+    reduce_half(0)
+    send_z(0)
     sum_own(1, 0)
 
     lane2 = iota2((192, 768), 1)
@@ -331,34 +358,6 @@
     gain_lanes2[...] = jnp.broadcast_to(0.5 * place_exact(gain2[...], jnp.where(
         channel_of(iota2((96, 640), 1)) == iota2((96, 640), 0), 1.0, 0.0).astype(BF16)), (8, 640))
 
-    def reduce_half(half):
-        when(has_down, ups[half].wait_recv)
-        when(has_up, downs[half].wait_recv)
-        total = own_sum[half] + part_in[0, half].astype(F32) + part_in[1, half].astype(F32)
-        total = total.astype(BF16).astype(F32)
-        spot_in_block = iota2((64, 128), 0) % 8
-        wide = []
-        for f in range(2):
-            cell = total[64 * f:64 * f + 64]
-            edge = jnp.where(spot_in_block < 4, shift_down(cell[:, 256:384]), shift_up(cell[:, 0:128]))
-            wide.append(jnp.concatenate([cell, edge], 1).reshape(z_total, 8, 512))
-        z_out[half] = jnp.concatenate(wide, 1).astype(BF16)
-
-    def z_copy(half, step, arriving):
-        other, who = z_partner(step)
-        here = (z - step + z_total) % z_total
-        slot = half * z_total + step
-        return pltpu.make_async_remote_copy(
-            src_ref=z_out.at[half, other], dst_ref=z_in.at[half, here if arriving else z],
-            send_sem=z_send.at[slot], recv_sem=z_recv.at[slot], device_id=who, device_id_type=MESH)
-
-    def send_z(half):
-        for step in range(1, z_total):
-            z_copy(half, step, False).start()
-        z_in[half, z] = z_out[half, z]
-
-    reduce_half(0)
-    send_z(0)
     reduce_half(1)
     send_z(1)
 
@@ -465,7 +464,7 @@
             vmem((4, 2, 128, 384)), vmem((1, 96), F32), vmem((9, 288, 96)), vmem((3, 288, 96)),
             vmem((1, 96), F32), vmem((9, 288, 192)), vmem((96, 192)),
             vmem((768, 384)), vmem((1280, 640)), vmem((8, 640), F32),
-            vmem((6, 2, 128, 384)), vmem((6, 2, 2, 64, 768)), vmem((4, 2, 2, 64, 512)),
+            vmem((2, 2, 128, 384)), vmem((6, 2, 2, 64, 768)), vmem((4, 2, 2, 64, 512)),
             vmem((96, 1152)), vmem((3, 288, 1152), F32), vmem((5, 2816, 256)),
             vmem((2, 2, 128, 384)), vmem((2, 2, 128, 384)), vmem((2, 128, 384), F32),
             vmem((2, 8, 16, 512)), vmem((2, 8, 16, 512)),

time: 41.4 us -> 40 us (0.966)
  Pallas kernels: 39.5 us -> 37.9 us
    pallas_call x1, Pallas kernels: 39.5 us -> 37.9 us  [shards(): pl.pallas_call(functools.partial(encoder_kernel, sizes), out_shape=jax.Sh...]
where the time goes in v2:
time: 40 us; the launch traced here: 39.7 us
  Pallas kernels  37.9 us (95%)
  local copies, waits for them, and re-layouts  1.77 us (4%)
    pallas_call x1, Pallas kernels, shards(): pl.pallas_call(functools.partial(encoder_kernel, sizes), out_shape=jax.Sh...  37.9 us
    unnamed x1, local copies, waits for them, and re-layouts  1.77 us

profile of v2, /device:TPU:1, one launch (start us, length us, event | category | flops | bytes accessed | tf_op | source)
XLA Modules:
  0.0 39.7 jit_solution(16247748839693738620)
XLA Ops:
  0.0 37.9 %encoder.1 = bf16[2,4,32,768]{3,2,1,0:T(8,128)(2,1)} custom-call(bf16[4,2,128,384]{3,2,1,0:T(8,128)(2,1)} %bitcast.11, f32[1,96]{1,0:T(1,128)} %bitcast.14, bf16[9,288,96]{2,1,0:T(8,128)(2,1)} %bitcast.12, bf16[3,288,96]{2,1,0:T(8,128)(2,1)} %bitcast.13, f32[1,96]{1,0:T(1,128)} %bitcast.15, bf16[9,288,192]{2,1,0:T(8,128)(2,1)} %bitcast.10, ...), custom_call_target="tpu_custom_call" | custom-call | tf_op jit(solution)/shard_map/encoder/pallas_call | solution.py:458
  37.9 1.8 %copy.10 = bf16[2,4,32,1,768]{4,2,3,1,0:T(8,128)(2,1)} copy(bf16[2,4,32,1,768]{4,2,3,1,0:T(8,128)(2,1)} %bitcast.9) | data formatting | bytes 786432

commit v3 on v2

--- a/solution.py
+++ b/solution.py
@@ -242,7 +242,7 @@
                         result = term if result is None else result + term
             return result
 
-        start = pl.multiple_of(a * 768, 128)
+        start = a * 768
         for r in range(5):
             at = [total(r, [(j, c - j) for j in range(3) if 0 <= c - j <= 2]) for c in range(5)]
             beyond = -total(r, [(0, 2)])
@@ -252,7 +252,8 @@
                 w5[r, pl.ds(start + 96 * n, 96)] = jnp.concatenate([q0, q1], 1).astype(BF16)
         return carry
 
-    lax.fori_loop(0, 3, compose_step, 0)
+    for a in range(3):
+        compose_step(a, 0)
 
     def row_cells(t, r, with_video):
         pieces = [cells1[t + a:t + a + 2, r].reshape(256, 768) for a in range(3)]
@@ -302,7 +303,7 @@
             send_sem=z_send.at[slot], recv_sem=z_recv.at[slot], device_id=who, device_id_type=MESH)
 
     def send_z(half):
-        for step in range(1, z_total):
+        for step in sorted(range(1, z_total), key=lambda step: -min(step, z_total - step)):
             z_copy(half, step, False).start()
         z_in[half, z] = z_out[half, z]
 
@@ -387,7 +388,7 @@
                     yc_wide[n, pl.ds(f * 8 + source, 8, stride=16), :] = part
         for n in range(5):
             yc_out[half, :, :, 128 * n:128 * n + 128] = yc_wide[n].astype(BF16).reshape(8, 16, 128)
-        for step in range(1, square):
+        for step in sorted(range(1, square), key=lambda step: -min(step, square - step)):
             yc_copy(half, step, False).start()
         yc_in[half, spot] = yc_out[half, spot]
 

time: 40 us -> 39.7 us (level)
  no operation moved by 1% of the time
where the time goes in v3:
time: 39.7 us; the launch traced here: 39.5 us
  Pallas kernels  37.7 us (95%)
  local copies, waits for them, and re-layouts  1.77 us (4%)
    pallas_call x1, Pallas kernels, shards(): pl.pallas_call(functools.partial(encoder_kernel, sizes), out_shape=jax.Sh...  37.7 us
    unnamed x1, local copies, waits for them, and re-layouts  1.77 us

profile of v3, /device:TPU:1, one launch (start us, length us, event | category | flops | bytes accessed | tf_op | source)
XLA Modules:
  0.0 39.5 jit_solution(11783846339989662495)
XLA Ops:
  0.0 37.7 %encoder.1 = bf16[2,4,32,768]{3,2,1,0:T(8,128)(2,1)} custom-call(bf16[4,2,128,384]{3,2,1,0:T(8,128)(2,1)} %bitcast.11, f32[1,96]{1,0:T(1,128)} %bitcast.14, bf16[9,288,96]{2,1,0:T(8,128)(2,1)} %bitcast.12, bf16[3,288,96]{2,1,0:T(8,128)(2,1)} %bitcast.13, f32[1,96]{1,0:T(1,128)} %bitcast.15, bf16[9,288,192]{2,1,0:T(8,128)(2,1)} %bitcast.10, ...), custom_call_target="tpu_custom_call" | custom-call | tf_op jit(solution)/shard_map/encoder/pallas_call | solution.py:459
  37.7 1.8 %copy.10 = bf16[2,4,32,1,768]{4,2,3,1,0:T(8,128)(2,1)} copy(bf16[2,4,32,1,768]{4,2,3,1,0:T(8,128)(2,1)} %bitcast.9) | data formatting | bytes 786432

commit v4 on v3

--- a/solution.py
+++ b/solution.py
@@ -374,9 +374,10 @@
     line8 = iota2((8, 128), 0)
 
     def relay(half):
-        for step in range(1, z_total):
-            z_copy(half, step, True).wait_recv()
-        for source in range(z_total):
+        for turn in range(z_total):
+            source = (z - turn + z_total) % z_total
+            if turn:
+                z_copy(half, turn, True).wait_recv()
             cells = z_in[half, source].astype(F32)
             for f in range(2):
                 cell = cells[8 * f:8 * f + 8]
@@ -396,9 +397,10 @@
     relay(1)
 
     def norm_second(half, t):
-        for step in range(1, square):
-            yc_copy(half, step, True).wait_recv()
-        for source in range(square):
+        for turn in range(square):
+            source = (spot - turn + square) % square
+            if turn:
+                yc_copy(half, turn, True).wait_recv()
             cells = yc_in[half, source].astype(F32)
             start = (source % clip_total) * row_total + source // clip_total
             for f in range(2):

time: 39.7 us -> 39.7 us (level)
  no operation moved by 1% of the time
where the time goes in v4:
time: 39.7 us; the launch traced here: 39.5 us
  Pallas kernels  37.7 us (95%)
  local copies, waits for them, and re-layouts  1.77 us (4%)
    pallas_call x1, Pallas kernels, shards(): pl.pallas_call(functools.partial(encoder_kernel, sizes), out_shape=jax.Sh...  37.7 us
    unnamed x1, local copies, waits for them, and re-layouts  1.77 us

profile of v4, /device:TPU:1, one launch (start us, length us, event | category | flops | bytes accessed | tf_op | source)
XLA Modules:
  0.0 39.5 jit_solution(7659094032414564106)
XLA Ops:
  0.0 37.7 %encoder.1 = bf16[2,4,32,768]{3,2,1,0:T(8,128)(2,1)} custom-call(bf16[4,2,128,384]{3,2,1,0:T(8,128)(2,1)} %bitcast.11, f32[1,96]{1,0:T(1,128)} %bitcast.14, bf16[9,288,96]{2,1,0:T(8,128)(2,1)} %bitcast.12, bf16[3,288,96]{2,1,0:T(8,128)(2,1)} %bitcast.13, f32[1,96]{1,0:T(1,128)} %bitcast.15, bf16[9,288,192]{2,1,0:T(8,128)(2,1)} %bitcast.10, ...), custom_call_target="tpu_custom_call" | custom-call | tf_op jit(solution)/shard_map/encoder/pallas_call | solution.py:461
  37.7 1.8 %copy.10 = bf16[2,4,32,1,768]{4,2,3,1,0:T(8,128)(2,1)} copy(bf16[2,4,32,1,768]{4,2,3,1,0:T(8,128)(2,1)} %bitcast.9) | data formatting | bytes 786432
